TPU v7x, 128 devices: a whole 4x4x4 slice. The times are simulated.
128 devices in a mesh: tm: 4 (over z), chan: 32 (over y, x, core).
Axes of the slice: x: 4, y: 4, z: 4, core: 2. Of those that a mesh axis runs over, the one named last changes fastest.
Arguments:
- records: bfloat16 [16384, 8192], P(('tm', 'chan')), may hold values from -600 to 600
- segment_keep: int32 [16, 256], P('tm', 'chan'), may hold values 0 or 1
Outputs:
- cross: bfloat16 [2, 96, 17, 32, 8192], P(None, 'tm', None, None, 'chan')
All inputs are finite; a program needn't handle non-finite values. No bound on the sum of `segment_keep` on one device may be relied on, other than what follows from the above.
Results may differ from a plain program's by a relative error of at most 0.007.
Values may be sent and summed in bfloat16 or wider, within the bound.
A program may use at most 320 MiB of HBM per device.

v0:
```python
import functools
import math

import jax
import jax.numpy as jnp
import numpy as np
from jax import lax
from jax.experimental import pallas as pl
from jax.experimental.pallas import tpu as pltpu
from jax.sharding import PartitionSpec as P

MESH = pl.DeviceIdType.MESH

L = 1024
FLO = 10
F = 96
BLK = 32
REACH = 8
NOFF = 2 * REACH + 1
SEG = 16

NZ = 4
NY = 4
NX = 4
NC = 2
FSHARE = F // NZ
FG = 8
GROUPS = FSHARE // FG
PIECE = 2 * FSHARE
CH = 256
ROWS = 128
HALF = 128

STAGES = ((2, 0, 256), (1, 0, 256), (3, 0, 256), (0, 0, 256))
NS = len(STAGES)
AHEAD = 2
LAG = 1

LINE = tuple((dx, dc) for dx in (1, 3, 0) for dc in (0, 1) if (dx, dc) != (0, 0))


def taper_table():
    t = np.arange(L, dtype=np.int64)
    k = FLO + np.arange(F, dtype=np.int64)
    phase = 2.0 * math.pi * ((k[:, None] * t[None, :]) % L) / L
    taper = (0.5 - 0.5 * np.cos(2.0 * math.pi * t / L)) / math.sqrt(3.0 * L / 8.0)
    both = np.stack([np.cos(phase) * taper, -np.sin(phase) * taper])
    both = both.reshape(2, NZ, GROUPS, FG, L).transpose(1, 2, 0, 3, 4)
    return both.reshape(2 * F, L).astype(np.float32).astype(jnp.bfloat16)


def chan_of(y, x, c):
    return (y * NX + x) * NC + c


def spectra_kernel(
    rec, keep, table_hbm, own, left, right,
    near, helped, partial, summed, spec, table, kown, kbuf,
    load, a_send, a_recv, a_local, p_send, p_recv,
    b_send, b_recv, b_local, c_send, c_recv, k_send, k_recv,
):
    z = lax.axis_index("tm")
    ch = lax.axis_index("chan")
    y = ch // (NX * NC)
    x = lax.rem(ch // NC, NX)
    c = lax.rem(ch, NC)
    nchan = NY * NX * NC
    after = lax.rem(ch + 1, nchan)
    before = lax.rem(ch + nchan - 1, nchan)

    def side(core):
        return 1 - 2 * core

    def along(steps):
        return lax.rem(x + NX + steps, NX)

    ahead, behind = along(side(c)), along(-side(c))

    load_table = pltpu.make_async_copy(table_hbm, table, load)
    load_table.start()

    barrier = pltpu.get_barrier_semaphore()
    signals = 0
    for dx, dc in LINE:
        peer = chan_of(y, lax.rem(x + dx, NX), lax.rem(c + dc, NC))
        pl.semaphore_signal(barrier, inc=1, device_id=(z, peer), device_id_type=MESH)
        signals += 1
    for dy in range(NY):
        for dz in range(NZ):
            if dy or dz:
                pl.semaphore_signal(
                    barrier, inc=1,
                    device_id=(lax.rem(z + dz, NZ), chan_of(lax.rem(y + dy, NY), x, c)),
                    device_id_type=MESH,
                )
                signals += 1
    for neighbour in (after, before):
        pl.semaphore_signal(barrier, inc=1, device_id=(z, neighbour), device_id_type=MESH)
        signals += 1

    pl.semaphore_wait(barrier, signals)

    def rows_of(group_x, group_c, j):
        dy, first, width = STAGES[j]
        column = chan_of(lax.rem(y + dy, NY), group_x, group_c) * CH + first
        return rec.at[:, pl.ds(pl.multiple_of(column, HALF), width)]

    def place(buffer, j, part):
        rows = pl.ds(pl.multiple_of(part * NC * ROWS + c * ROWS, ROWS), ROWS)
        return buffer.at[j, rows, pl.ds(0, STAGES[j][2])]

    def gather(j):
        to_helped, to_near = [], []
        n = 0
        for e in (0, 1):
            core = lax.rem(c + e, NC)
            s = side(core)
            for copies, buffer, part, group_x, target_x in (
                (to_helped, helped, 1, along(2), along(-s)),
                (to_near, near, 1, along(s), along(s)),
                (to_helped, helped, 0, along(-s), x),
                (to_near, near, 0, x, x),
            ):
                source, target = rows_of(group_x, core, j), place(buffer, j, part)
                if part == 0 and e == 0:
                    copy = pltpu.make_async_copy(
                        source, target, a_local.at[j, 0 if buffer is helped else 1]
                    )
                else:
                    copy = pltpu.make_async_remote_copy(
                        src_ref=source,
                        dst_ref=target,
                        send_sem=a_send.at[j, n],
                        recv_sem=a_recv.at[j, n],
                        device_id=(z, chan_of(y, target_x, core)),
                        device_id_type=MESH,
                    )
                    n += 1
                copy.start()
                copies.append((copy, part == 0 and e == 0))
        return to_helped, to_near

    gathers = [gather(j) for j in range(AHEAD)]
    lane_block = lax.broadcasted_iota(jnp.int32, (1, CH), 1) // BLK
    for s in range(NZ):
        spread = jnp.zeros((1, CH), jnp.int32)
        for b in range(CH // BLK):
            spread = jnp.where(lane_block == b, keep[s, b], spread)
        kown[s : s + 1, :] = spread.astype(jnp.float32)
    kown[NY:8, :] = jnp.zeros((8 - NY, CH), jnp.float32)
    keeps = []
    for n, ky in enumerate((1, 2, 3)):
        copy = pltpu.make_async_remote_copy(
            src_ref=kown,
            dst_ref=kbuf.at[y],
            send_sem=k_send.at[n],
            recv_sem=k_recv.at[n],
            device_id=(z, chan_of(lax.rem(y + ky, NY), x, c)),
            device_id_type=MESH,
        )
        copy.start()
        keeps.append(copy)

    def half_sum(buffer, j, chips):
        width = STAGES[j][2]
        total = jnp.zeros((2 * F, width), jnp.float32)
        energy = jnp.zeros((1, width), jnp.float32)
        for part, chip in enumerate(chips):
            data = buffer[j, part * NC * ROWS : (part + 1) * NC * ROWS, 0:width]
            columns = pl.ds(pl.multiple_of(chip * (NC * ROWS), NC * ROWS), NC * ROWS)
            total = total + jnp.dot(table[:, columns], data, preferred_element_type=jnp.float32)
            wide = data.astype(jnp.float32)
            energy = energy + jnp.sum(wide * wide, axis=0, keepdims=True)
        return total, energy

    def arrive(copies):
        for copy, local in copies:
            copy.wait() if local else copy.wait_recv()

    def pass_on(j):
        arrive(gathers[j][0])
        if len(gathers) < NS:
            gathers.append(gather(len(gathers)))
        total, energy = half_sum(helped, j, (x, ahead))
        width = STAGES[j][2]
        partial[j, 0 : 2 * F, 0:width] = total
        partial[j, 2 * F :, 0:width] = jnp.broadcast_to(energy, (8, width))
        copy = pltpu.make_async_remote_copy(
            src_ref=partial.at[j, :, pl.ds(0, width)],
            dst_ref=summed.at[j, :, pl.ds(0, width)],
            send_sem=p_send.at[j],
            recv_sem=p_recv.at[j],
            device_id=(z, chan_of(y, behind, c)),
            device_id_type=MESH,
        )
        copy.start()
        passed.append(copy)

    def halo(j):
        dy, first, width = STAGES[j]
        source = lax.rem(y + NY - dy, NY)
        copies = []
        for n, (neighbour, into) in enumerate(((after, left), (before, right))):
            copy = pltpu.make_async_remote_copy(
                src_ref=own.at[source, :, :, pl.ds(first, width)],
                dst_ref=into.at[source, :, :, pl.ds(first, width)],
                send_sem=c_send.at[j, n],
                recv_sem=c_recv.at[j, n],
                device_id=(z, neighbour),
                device_id_type=MESH,
            )
            copy.start()
            copies.append(copy)
        return copies

    def spread_arrived(j):
        for copy, local in spreads[j]:
            copy.wait() if local else copy.wait_recv()

    def finish(j):
        dy, first, width = STAGES[j]
        q = lax.rem(y + dy, NY)
        arrive(gathers[j][1])
        total, energy = half_sum(near, j, (x, behind))
        passed[j].wait_recv()
        for i in range(len(halos), j - 1):
            spread_arrived(i)
            halos.append(halo(i))
        energy = energy + summed[j, 2 * F : 2 * F + 1, 0:width]
        lanes = slice(first, first + width)
        kept = kown[pl.ds(y, 1), lanes] if dy == 0 else kbuf[q, pl.ds(y, 1), lanes]
        scale = lax.rsqrt(energy * (1.0 / L) + 1e-06) * kept
        raw = total + summed[j, 0 : 2 * F, 0:width]
        spec[j, :, :, 0:width] = (raw * scale).astype(jnp.bfloat16).reshape(NZ, PIECE, width)
        sent = []
        for dz in (2, 1, 3, 0):
            pz = lax.rem(z + dz, NZ)
            source = spec.at[j, pz, :, pl.ds(0, width)]
            target = own.at[y, z, :, pl.ds(first, width)]
            if dy == 0 and dz == 0:
                copy = pltpu.make_async_copy(source, target, b_local.at[j])
            else:
                copy = pltpu.make_async_remote_copy(
                    src_ref=source,
                    dst_ref=target,
                    send_sem=b_send.at[j, dz],
                    recv_sem=b_recv.at[j, dz],
                    device_id=(pz, chan_of(q, x, c)),
                    device_id_type=MESH,
                )
            copy.start()
            sent.append((copy, dy == 0 and dz == 0))
        spreads.append(sent)

    load_table.wait()
    passed, spreads, halos = [], [], []
    for j in range(NS):
        pass_on(j)
        if j == 0:
            for copy in keeps:
                copy.wait_recv()
        if j >= LAG:
            finish(j - LAG)
    for j in range(NS - LAG, NS):
        finish(j)
    for j in range(len(halos), NS):
        spread_arrived(j)
        halos.append(halo(j))

    for stage in gathers:
        for copies in stage:
            for copy, local in copies:
                if not local:
                    copy.wait_send()
    for copy in keeps + passed:
        copy.wait_send()
    for sent in spreads:
        for copy, local in sent:
            if not local:
                copy.wait_send()
    for pair in halos:
        for copy in pair:
            copy.wait()

    @pl.when(ch == 0)
    def _():
        left[...] = jnp.zeros_like(left)

    @pl.when(ch == nchan - 1)
    def _():
        right[...] = jnp.zeros_like(right)


def gather_spectra(records, keep, table):
    window = jax.ShapeDtypeStruct((NY, NZ, PIECE, CH), jnp.bfloat16)
    vmem = pl.BlockSpec(memory_space=pltpu.VMEM)
    hbm = pl.BlockSpec(memory_space=pl.ANY)
    dma = pltpu.SemaphoreType.DMA
    half = pltpu.VMEM((NS, 2 * NC * ROWS, CH), jnp.bfloat16)
    sums = pltpu.VMEM((NS, 2 * F + 8, CH), jnp.float32)
    return pl.pallas_call(
        spectra_kernel,
        out_shape=(window, window, window),
        in_specs=[hbm, pl.BlockSpec(memory_space=pltpu.SMEM), hbm],
        out_specs=(vmem, vmem, vmem),
        scratch_shapes=[
            half, half, sums, sums,
            pltpu.VMEM((NS, NZ, PIECE, CH), jnp.bfloat16),
            pltpu.VMEM((2 * F, L), jnp.bfloat16),
            pltpu.VMEM((8, CH), jnp.float32),
            pltpu.VMEM((NY, 8, CH), jnp.float32),
            dma, dma((NS, 6)), dma((NS, 6)), dma((NS, 2)), dma((NS,)), dma((NS,)),
            dma((NS, NZ)), dma((NS, NZ)), dma((NS,)),
            dma((NS, 2)), dma((NS, 2)), dma((NY - 1,)), dma((NY - 1,)),
        ],
        compiler_params=pltpu.CompilerParams(
            collective_id=0, has_side_effects=True, vmem_limit_bytes=211 << 18
        ),
        cost_estimate=pl.CostEstimate(
            flops=2 * 2 * F * L * NY * CH, bytes_accessed=2 * NY * L * CH, transcendentals=0
        ),
        name="gather_spectra",
    )(records, keep, table)


def cross_kernel(own, left, right, out, turned, weights, made, sem):
    terms = SEG * 2 * FG
    reach = NOFF * BLK + HALF - BLK
    lane_block = lax.broadcasted_iota(jnp.int32, (BLK, HALF), 1) // BLK
    row = lax.rem(lax.broadcasted_iota(jnp.int32, (terms, HALF), 0), FG)

    def group(g, carry):
        for w, window in enumerate((left, own, right)):
            rows = window[:, :, pl.ds(pl.multiple_of(g * 2 * FG, 2 * FG), 2 * FG), :].reshape(terms, CH)
            turned[w * CH : (w + 1) * CH, :] = rows.T
            if w == 1:
                wide = (rows.astype(jnp.float32) * (1.0 / SEG)).reshape(SEG, 2, FG, CH)
                plain = wide.reshape(terms, CH).astype(jnp.bfloat16)
                swapped = jnp.stack([wide[:, 1], -wide[:, 0]], 1)
                swapped = swapped.reshape(terms, CH).astype(jnp.bfloat16)
                for h in range(2):
                    weights[h, :, 0:HALF] = plain[:, h * HALF : (h + 1) * HALF]
                    weights[h, :, HALF : 2 * HALF] = swapped[:, h * HALF : (h + 1) * HALF]
        for f8 in range(FG):
            f = g * FG + f8
            chosen = jnp.where(row == f8, 1.0, 0.0).astype(jnp.bfloat16)
            chosen = jnp.concatenate([chosen, chosen], 1)
            for h in range(2):
                product = jnp.dot(
                    turned[h * HALF : h * HALF + reach, :],
                    weights[h] * chosen,
                    preferred_element_type=jnp.float32,
                )
                for part in range(2):
                    side = product[:, part * HALF : (part + 1) * HALF]
                    blocks = [side[r : r + BLK] for r in range(0, reach, BLK)]
                    for k in range(NOFF):
                        picked = blocks[k]
                        for i in range(1, HALF // BLK):
                            picked = jnp.where(lane_block == i, blocks[k + i], picked)
                        made[part, f, k, :, h * HALF : (h + 1) * HALF] = picked.astype(jnp.bfloat16)
            pltpu.make_async_copy(made.at[:, pl.ds(f, 1)], out.at[:, pl.ds(f, 1)], sem).start()
        return carry

    lax.fori_loop(0, GROUPS, group, 0)
    pltpu.make_async_copy(made, out, sem).wait()


def cross_products(own, left, right):
    terms = SEG * 2 * FG
    vmem = pl.BlockSpec(memory_space=pltpu.VMEM)
    result = (2, FSHARE, NOFF, BLK, CH)
    return pl.pallas_call(
        cross_kernel,
        out_shape=jax.ShapeDtypeStruct(result, jnp.bfloat16),
        in_specs=[vmem, vmem, vmem],
        out_specs=pl.BlockSpec(memory_space=pl.ANY),
        scratch_shapes=[
            pltpu.VMEM((3 * CH, terms), jnp.bfloat16),
            pltpu.VMEM((2, terms, 2 * HALF), jnp.bfloat16),
            pltpu.VMEM(result, jnp.bfloat16),
            pltpu.SemaphoreType.DMA,
        ],
        compiler_params=pltpu.CompilerParams(vmem_limit_bytes=48 << 20),
        name="cross_products",
    )(own, left, right)


def shards(table, records, segment_keep):
    own, left, right = gather_spectra(records, segment_keep, table)
    return cross_products(own, left, right)


def solution(mesh):
    in_specs = (P(None, None), P(("tm", "chan"), None), P("tm", "chan"))
    out_specs = P(None, "tm", None, None, "chan")
    call = jax.shard_map(
        shards, mesh=mesh, in_specs=in_specs, out_specs=out_specs, check_vma=False
    )
    table = taper_table()

    def run(records, segment_keep):
        return call(jnp.asarray(table), records, segment_keep)

    return run
```

profile of v0, /device:TPU:1, one launch (start us, length us, event | category | flops | bytes accessed | tf_op | source)
XLA Modules:
  0.0 46.7 jit_solution(11797589016083234682)
XLA Ops:
  0.0 0.0 copy-start
  0.0 0.7 %copy-done = s32[4,8]{1,0:T(4,128)S(1)} copy-done((s32[4,8]{1,0:T(4,128)S(1)}, s32[4,8]{1,0:T(4,128)}, u32[]{:S(2)}) %copy-start) | copy-done | bytes 152
  0.7 39.7 %gather_spectra.1 = (bf16[4,4,48,256]{3,2,1,0:T(8,128)(2,1)S(1)}, bf16[4,4,48,256]{3,2,1,0:T(8,128)(2,1)S(1)}, bf16[4,4,48,256]{3,2,1,0:T(8,128)(2,1)S(1)}) custom-call(bf16[128,8192]{1,0:T(8,128)(2,1)} %rec.1, s32[4,8]{1,0:T(4,128)S(1)} %copy-done, bf16[192,1024]{1,0:T(8,128)(2,1)} %constant.2.clone.table_hbm), custom_call_target="tpu_custom_call" | custom-call | flops 402653184 | bytes 2097152 | tf_op jit(solution)/shard_map/gather_spectra/pallas_call | solution.py:301
  40.4 6.3 %cross_products.1 = bf16[2,24,17,32,256]{4,3,2,1,0:T(8,128)(2,1)} custom-call(bf16[4,4,48,256]{3,2,1,0:T(8,128)(2,1)S(1)} %get-tuple-element.8.own, bf16[4,4,48,256]{3,2,1,0:T(8,128)(2,1)S(1)} %get-tuple-element.9.left, bf16[4,4,48,256]{3,2,1,0:T(8,128)(2,1)S(1)} %get-tuple-element.10.right), custom_call_target="tpu_custom_call" | custom-call | tf_op jit(solution)/shard_map/cross_products/pallas_call | solution.py:373
Async XLA Ops:
  0.0 0.7 %copy-start = (s32[4,8]{1,0:T(4,128)S(1)}, s32[4,8]{1,0:T(4,128)}, u32[]{:S(2)}) copy-start(s32[4,8]{1,0:T(4,128)} %keep.1) | copy-start | bytes 388
where the time goes:
time: 46.8 us; the launch traced here: 46.7 us
  Pallas kernels  46 us (98%)
  local copies, waits for them, and re-layouts  0.68 us (1%)
    pallas_call x1, Pallas kernels, gather_spectra(): pl.pallas_call(spectra_kernel, out_shape=(window, window, window), in_spe...  39.7 us
    pallas_call x1, Pallas kernels, cross_products(): pl.pallas_call(cross_kernel, out_shape=jax.ShapeDtypeStruct(result, jnp.b...  6.28 us

commit v1 on v0

--- a/solution.py
+++ b/solution.py
@@ -223,9 +223,6 @@
         arrive(gathers[j][1])
         total, energy = half_sum(near, j, (x, behind))
         passed[j].wait_recv()
-        for i in range(len(halos), j - 1):
-            spread_arrived(i)
-            halos.append(halo(i))
         energy = energy + summed[j, 2 * F : 2 * F + 1, 0:width]
         lanes = slice(first, first + width)
         kept = kown[pl.ds(y, 1), lanes] if dy == 0 else kbuf[q, pl.ds(y, 1), lanes]
@@ -256,6 +253,9 @@
     passed, spreads, halos = [], [], []
     for j in range(NS):
         pass_on(j)
+        for i in range(len(halos), j - 2):
+            spread_arrived(i)
+            halos.append(halo(i))
         if j == 0:
             for copy in keeps:
                 copy.wait_recv()
@@ -329,26 +329,31 @@
     lane_block = lax.broadcasted_iota(jnp.int32, (BLK, HALF), 1) // BLK
     row = lax.rem(lax.broadcasted_iota(jnp.int32, (terms, HALF), 0), FG)
 
-    def group(g, carry):
+    def prepare(g):
         for w, window in enumerate((left, own, right)):
-            rows = window[:, :, pl.ds(pl.multiple_of(g * 2 * FG, 2 * FG), 2 * FG), :].reshape(terms, CH)
-            turned[w * CH : (w + 1) * CH, :] = rows.T
+            rows = window[:, :, g * 2 * FG : (g + 1) * 2 * FG, :].reshape(terms, CH)
+            turned[g, w * CH : (w + 1) * CH, :] = rows.T
             if w == 1:
                 wide = (rows.astype(jnp.float32) * (1.0 / SEG)).reshape(SEG, 2, FG, CH)
                 plain = wide.reshape(terms, CH).astype(jnp.bfloat16)
                 swapped = jnp.stack([wide[:, 1], -wide[:, 0]], 1)
                 swapped = swapped.reshape(terms, CH).astype(jnp.bfloat16)
                 for h in range(2):
-                    weights[h, :, 0:HALF] = plain[:, h * HALF : (h + 1) * HALF]
-                    weights[h, :, HALF : 2 * HALF] = swapped[:, h * HALF : (h + 1) * HALF]
+                    weights[g, h, :, 0:HALF] = plain[:, h * HALF : (h + 1) * HALF]
+                    weights[g, h, :, HALF : 2 * HALF] = swapped[:, h * HALF : (h + 1) * HALF]
+
+    prepare(0)
+    for g in range(GROUPS):
         for f8 in range(FG):
+            if f8 == FG // 2 and g + 1 < GROUPS:
+                prepare(g + 1)
             f = g * FG + f8
             chosen = jnp.where(row == f8, 1.0, 0.0).astype(jnp.bfloat16)
             chosen = jnp.concatenate([chosen, chosen], 1)
             for h in range(2):
                 product = jnp.dot(
-                    turned[h * HALF : h * HALF + reach, :],
-                    weights[h] * chosen,
+                    turned[g, h * HALF : h * HALF + reach, :],
+                    weights[g, h] * chosen,
                     preferred_element_type=jnp.float32,
                 )
                 for part in range(2):
@@ -360,9 +365,6 @@
                             picked = jnp.where(lane_block == i, blocks[k + i], picked)
                         made[part, f, k, :, h * HALF : (h + 1) * HALF] = picked.astype(jnp.bfloat16)
             pltpu.make_async_copy(made.at[:, pl.ds(f, 1)], out.at[:, pl.ds(f, 1)], sem).start()
-        return carry
-
-    lax.fori_loop(0, GROUPS, group, 0)
     pltpu.make_async_copy(made, out, sem).wait()
 
 
@@ -376,8 +378,8 @@
         in_specs=[vmem, vmem, vmem],
         out_specs=pl.BlockSpec(memory_space=pl.ANY),
         scratch_shapes=[
-            pltpu.VMEM((3 * CH, terms), jnp.bfloat16),
-            pltpu.VMEM((2, terms, 2 * HALF), jnp.bfloat16),
+            pltpu.VMEM((GROUPS, 3 * CH, terms), jnp.bfloat16),
+            pltpu.VMEM((GROUPS, 2, terms, 2 * HALF), jnp.bfloat16),
             pltpu.VMEM(result, jnp.bfloat16),
             pltpu.SemaphoreType.DMA,
         ],

time: 46.8 us -> 46.5 us (level)
  no operation moved by 1% of the time
where the time goes in v1:
time: 46.5 us; the launch traced here: 46.4 us
  Pallas kernels  45.7 us (98%)
  local copies, waits for them, and re-layouts  0.68 us (1%)
    pallas_call x1, Pallas kernels, gather_spectra(): pl.pallas_call(spectra_kernel, out_shape=(window, window, window), in_spe...  39.7 us
    pallas_call x1, Pallas kernels, cross_products(): pl.pallas_call(cross_kernel, out_shape=jax.ShapeDtypeStruct(result, jnp.b...  5.96 us

profile of v1, /device:TPU:1, one launch (start us, length us, event | category | flops | bytes accessed | tf_op | source)
XLA Modules:
  0.0 46.4 jit_solution(12337380635426781354)
XLA Ops:
  0.0 0.0 copy-start
  0.0 0.7 %copy-done = s32[4,8]{1,0:T(4,128)S(1)} copy-done((s32[4,8]{1,0:T(4,128)S(1)}, s32[4,8]{1,0:T(4,128)}, u32[]{:S(2)}) %copy-start) | copy-done | bytes 152
  0.7 39.7 %gather_spectra.1 = (bf16[4,4,48,256]{3,2,1,0:T(8,128)(2,1)S(1)}, bf16[4,4,48,256]{3,2,1,0:T(8,128)(2,1)S(1)}, bf16[4,4,48,256]{3,2,1,0:T(8,128)(2,1)S(1)}) custom-call(bf16[128,8192]{1,0:T(8,128)(2,1)} %rec.1, s32[4,8]{1,0:T(4,128)S(1)} %copy-done, bf16[192,1024]{1,0:T(8,128)(2,1)} %constant.2.clone.table_hbm), custom_call_target="tpu_custom_call" | custom-call | flops 402653184 | bytes 2097152 | tf_op jit(solution)/shard_map/gather_spectra/pallas_call | solution.py:301
  40.4 6.0 %cross_products.1 = bf16[2,24,17,32,256]{4,3,2,1,0:T(8,128)(2,1)} custom-call(bf16[4,4,48,256]{3,2,1,0:T(8,128)(2,1)S(1)} %get-tuple-element.8.own, bf16[4,4,48,256]{3,2,1,0:T(8,128)(2,1)S(1)} %get-tuple-element.9.left, bf16[4,4,48,256]{3,2,1,0:T(8,128)(2,1)S(1)} %get-tuple-element.10.right), custom_call_target="tpu_custom_call" | custom-call | tf_op jit(solution)/shard_map/cross_products/pallas_call | solution.py:375
Async XLA Ops:
  0.0 0.7 %copy-start = (s32[4,8]{1,0:T(4,128)S(1)}, s32[4,8]{1,0:T(4,128)}, u32[]{:S(2)}) copy-start(s32[4,8]{1,0:T(4,128)} %keep.1) | copy-start | bytes 388
